TPU v7x, 32 devices: a whole 2x2x4 slice. The times are simulated.
32 devices in a mesh: slab: 2 (over x), plane: 8 (over z, y), brick: 2 (over core).
Axes of the slice: x: 2, y: 2, z: 4, core: 2. Of those that a mesh axis runs over, the one named last changes fastest.
Arguments:
- camera_rows: bfloat16 [4, 16, 32, 2048], P(None, 'slab', ('plane', 'brick')), parts along dimension 1, may hold values from 0.19921875 to 5
- estimate: float32 [16, 32, 2048], P('slab', None, ('plane', 'brick')), parts along dimension 0, may hold values from 0.2 to 5
- psf_bank: float32 [32, 4, 3, 31], P(('slab', 'plane', 'brick')), parts along dimension 0, may hold values from 0 to 1.25, as said below
- psf_owner: int32 [32], P('slab'), parts along dimension 0, may hold values from 0 to 15, each once
- view_mask: int32 [32, 4], P('slab'), parts along dimension 0, may hold values 0 or 1
Outputs:
- deconvolved: float32 [16, 32, 2048], P('slab', None, ('plane', 'brick')), parts along dimension 0
There are 2 independent parts, one for each index of `slab`. A program takes and returns all parts, laid end to end along the dimension named above; each array names one. Nothing has to cross between parts.
Inputs may be any that keep to these rules, and one draw needn't show every extreme that they name: `psf_owner`: every brick names a different device: the map is a permutation of 0 to 15. `psf_bank`: every tap is positive.
All inputs are finite; a program needn't handle non-finite values.
Results may differ from a plain program's by a relative error of at most 0.0003.
Values may be sent and summed in bfloat16 or wider, within the bound.
A program may use at most 192 MiB of HBM per device.

v0:
```python
import jax
import jax.numpy as jnp
from jax import lax
from jax.sharding import PartitionSpec as P

V = 4
RADIUS = 15
ITERS = 2
BACKGROUND = 0.1
HIGHEST = lax.Precision.HIGHEST


def padded_2(cells, sides, width):
    for axis, dim in sides:
        count = lax.axis_size(axis)
        ends = count - 1
        head = lax.slice_in_dim(cells, 0, width, axis=dim)
        tail = lax.slice_in_dim(cells, cells.shape[dim] - width, cells.shape[dim], axis=dim)
        cells = jnp.concatenate(
            [
                lax.ppermute(tail, axis, [(i, (i + 1) % count) for i in range(ends)]),
                cells,
                lax.ppermute(head, axis, [((i + 1) % count, i) for i in range(ends)]),
            ],
            axis=dim,
        )
    return cells


def banded(profiles, size_in, size_out, offset):
    tap_count = profiles.shape[-1]
    centre = tap_count // 2
    lag_index = (
        jnp.arange(size_in, dtype=jnp.int32)[:, None]
        - jnp.arange(size_out, dtype=jnp.int32)[None, :]
        - offset
        + centre
    )
    one_hot = (
        lag_index[:, :, None] == jnp.arange(tap_count, dtype=jnp.int32)[None, None, :]
    ).astype(jnp.float32)
    return jnp.einsum("ijt,vt->vij", one_hot, profiles, precision=HIGHEST)


def across_columns(volume, band_x):
    if volume.ndim == 3:
        return jnp.einsum("zyi,vij->vzyj", volume, band_x, precision=HIGHEST)
    return jnp.einsum("vzyi,vij->vzyj", volume, band_x, precision=HIGHEST)


def across_rows(volume, band_y):
    view_count, depth_count, row_count, col_count = volume.shape
    block_rows = band_y.shape[2]
    margin = (band_y.shape[1] - block_rows) // 2
    pieces = volume.reshape(view_count, depth_count, row_count // block_rows, block_rows, col_count)
    blanks = jnp.zeros((view_count, depth_count, 1, margin, col_count), jnp.float32)
    before = jnp.concatenate([blanks, pieces[:, :, :-1, block_rows - margin :, :]], axis=2)
    behind = jnp.concatenate([pieces[:, :, 1:, :margin, :], blanks], axis=2)
    windows = jnp.concatenate([before, pieces, behind], axis=3)
    result = jnp.einsum("vzqic,vij->vzqjc", windows, band_y, precision=HIGHEST)
    return result.reshape(view_count, depth_count, row_count, col_count)


def across_depth(volume, band_z):
    return jnp.einsum("vzyc,vzw->vwyc", volume, band_z, precision=HIGHEST)


def separable(volume, bands):
    return across_depth(across_rows(across_columns(volume, bands[0]), bands[1]), bands[2])


def shards(camera_rows, estimate, psf_bank, psf_owner, view_mask):
    regrouped = lax.all_to_all(
        camera_rows, ("plane", "brick"), split_axis=3, concat_axis=2, tiled=True
    )
    position = lax.axis_index(("plane", "brick"))
    brick_ids = jnp.arange(psf_owner.shape[0], dtype=jnp.int32)
    is_mine = brick_ids == position
    owner_id = jnp.sum(jnp.where(is_mine, psf_owner, 0))
    observed = jnp.sum(jnp.where(is_mine[:, None], view_mask, 0), axis=0) > 0
    fitted = lax.all_gather(psf_bank, ("plane", "brick"), axis=0, tiled=True)
    chosen = (brick_ids == owner_id).astype(jnp.float32)
    kernels = jnp.einsum("b,bvat->vat", chosen, fitted, precision=HIGHEST)
    kernels = kernels / jnp.sum(kernels, axis=-1, keepdims=True)
    flipped = kernels[:, :, ::-1]
    depth_size = estimate.shape[0]
    row_size = estimate.shape[1]
    col_size = estimate.shape[2]
    block_size = 128 if row_size % 128 == 0 else row_size

    def make_bands(profiles):
        return (
            banded(profiles[:, 2], col_size + 2 * RADIUS, col_size, RADIUS),
            banded(profiles[:, 1], block_size + 2 * RADIUS, block_size, RADIUS),
            banded(profiles[:, 0], depth_size, depth_size, 0),
        )

    blur_bands = make_bands(kernels)
    back_bands = make_bands(flipped)
    current = estimate
    for iteration in range(ITERS):
        padded = padded_2(current.astype(jnp.bfloat16), ((("plane", "brick"), 2),), RADIUS).astype(
            current.dtype
        )
        blurred = separable(padded, blur_bands)
        quotient = jnp.where(
            observed[:, None, None, None],
            regrouped.astype(jnp.float32) / (blurred + BACKGROUND),
            0.0,
        )
        quotient_wide = padded_2(
            quotient.astype(jnp.bfloat16), ((("plane", "brick"), 3),), RADIUS
        ).astype(quotient.dtype)
        corrected = separable(quotient_wide, back_bands)
        factor = jnp.sum(jnp.where(observed[:, None, None, None], corrected, 1.0), axis=0) / V
        current = current * factor
    return current


def solution(mesh):
    return jax.shard_map(
        shards,
        mesh=mesh,
        in_specs=(
            P(None, "slab", ("plane", "brick"), None),
            P("slab", None, ("plane", "brick")),
            P(("slab", "plane", "brick"), None, None, None),
            P("slab"),
            P("slab", None),
        ),
        out_specs=P("slab", None, ("plane", "brick")),
        check_vma=False,
    )
```

profile of v0, /device:TPU:1, one launch (start us, length us, event | category | flops | bytes accessed | tf_op | source)
XLA Modules:
  0.0 100.3 jit_solution(6253015987272240798)
XLA Ops:
  0.0 6.3 %copy.47 = bf16[4,8,2,2048]{1,0,2,3:T(4,128)(2,1)} copy(bf16[4,8,2,2048]{3,2,1,0:T(2,128)(2,1)} %param.5) | data formatting | bytes 524288 | tf_op args[0]
  6.4 6.5 %reshape.127 = bf16[16,2,4096]{2,1,0:T(2,128)(2,1)} reshape(bf16[2048,2,4,8]{3,2,1,0:T(4,128)(2,1)} %bitcast.116) | data formatting | bytes 524288
  12.8 7.3 %all-to-all-start = ((bf16[16,2,4096]{2,1,0:T(2,128)(2,1)}), bf16[16,2,4096]{2,1,0:T(2,128)(2,1)S(1)}, u32[]{:S(2)}, u32[]{:S(2)}) async-start(bf16[16,2,4096]{2,1,0:T(2,128)(2,1)} %reshape.127), calls=%async_computation | async-start | bytes 524288 | tf_op jit(solution)/shard_map/all_to_all | solution.py:73
  20.3 2.0 %collective-permute-start.1 = (bf16[8,32,15]{2,1,0:T(8,128)(2,1)S(1)}, bf16[8,32,15]{2,1,0:T(8,128)(2,1)S(1)}, u32[]{:S(2)}, u32[]{:S(2)}) collective-permute-start(bf16[8,32,15]{2,1,0:T(8,128)(2,1)S(1)} %get-tuple-element.12), channel_id=1, source_target_pairs={{1,0},{2,1},{3,2},{4,3},{5,4},{6,5},{7,6},{8,7},{9,8},{10,9},{11,1... | collective-permute-start | bytes 23048 | tf_op jit(solution)/shard_map/ppermute | solution.py:23
  22.3 3.5 %collective-permute-start = (bf16[8,32,15]{2,1,0:T(8,128)(2,1)S(1)}, bf16[8,32,15]{2,1,0:T(8,128)(2,1)S(1)}, u32[]{:S(2)}, u32[]{:S(2)}) collective-permute-start(bf16[8,32,15]{2,1,0:T(8,128)(2,1)S(1)} %get-tuple-element.11), channel_id=1, source_target_pairs={{0,1},{1,2},{2,3},{3,4},{4,5},{5,6},{6,7},{7,8},{8,9},{9,10},{10,1... | collective-permute-start | bytes 23048 | tf_op jit(solution)/shard_map/ppermute | solution.py:21
  25.9 20.7 %all_gather.3 = f32[16,4,3,31]{3,1,2,0:T(4,128)S(1)} all-gather(f32[1,4,3,31]{3,1,2,0:T(4,128)S(1)} %copy-done.1), channel_id=1, replica_groups=mesh['slab'=2,'plane'=8,'brick'=2] {'plane','brick'}, dimensions={0}, use_global_device_ids=true | all-gather | bytes 25296 | tf_op jit(solution)/shard_map/all_gather | solution.py:81
  46.6 0.6 select_reduce_fusion.1
  47.2 0.8 fusion.48
  48.2 0.9 fusion.12
  49.1 0.3 convolution_bitcast_fusion.8
  49.4 0.1 select_reduce_fusion
  49.5 0.1 slice.54
  49.6 0.9 fusion.13
  50.5 0.1 slice.48
  50.6 0.3 convolution_bitcast_fusion.9
  50.9 0.4 convolution_bitcast_fusion.10
  51.3 0.1 slice.46
  51.5 0.5 convolution_bitcast_fusion.1
  52.0 0.7 convolution_bitcast_fusion.7
  52.7 5.9 %reshape.128 = bf16[2048,2,4,8]{3,2,1,0:T(4,128)(2,1)} reshape(bf16[16,2,4096]{2,1,0:T(2,128)(2,1)S(1)} %all-to-all-done) | data formatting | bytes 524288
  58.7 5.9 %copy.48 = f32[4,8,2,16,128]{4,1,2,3,0:T(8,128)S(1)} copy(bf16[4,8,2,16,128]{1,0,2,4,3:T(4,128)(2,1)} %bitcast.115) | data formatting | bytes 786432 | tf_op jit(solution)/shard_map/convert_element_type | solution.py:108
  64.6 0.9 fusion.8
  65.5 0.1 fusion.77
  65.6 2.1 %collective-permute-start.3 = (bf16[4,8,32,15]{3,1,2,0:T(8,128)(2,1)S(1)}, bf16[4,8,32,15]{3,1,2,0:T(8,128)(2,1)S(1)}, u32[]{:S(2)}, u32[]{:S(2)}) collective-permute-start(bf16[4,8,32,15]{3,1,2,0:T(8,128)(2,1)S(1)} %get-tuple-element.8), channel_id=1, source_target_pairs={{1,0},{2,1},{3,2},{4,3},{5,4},{6,5},{7,6},{8,7},{9,8},{10,9},{11,1... | collective-permute-start | bytes 92168 | tf_op jit(solution)/shard_map/ppermute | solution.py:23
  67.7 3.5 %collective-permute-start.2 = (bf16[4,8,32,15]{3,1,2,0:T(8,128)(2,1)S(1)}, bf16[4,8,32,15]{3,1,2,0:T(8,128)(2,1)S(1)}, u32[]{:S(2)}, u32[]{:S(2)}) collective-permute-start(bf16[4,8,32,15]{3,1,2,0:T(8,128)(2,1)S(1)} %get-tuple-element.7), channel_id=1, source_target_pairs={{0,1},{1,2},{2,3},{3,4},{4,5},{5,6},{6,7},{7,8},{8,9},{9,10},{10,1... | collective-permute-start | bytes 92168 | tf_op jit(solution)/shard_map/ppermute | solution.py:21
  71.2 0.4 convolution_bitcast_fusion.11
  71.7 1.6 %collective-permute-done.3 = bf16[4,8,32,15]{3,1,2,0:T(8,128)(2,1)S(1)} collective-permute-done((bf16[4,8,32,15]{3,1,2,0:T(8,128)(2,1)S(1)}, bf16[4,8,32,15]{3,1,2,0:T(8,128)(2,1)S(1)}, u32[]{:S(2)}, u32[]{:S(2)}) %collective-permute-start.3) | collective-permute-done | bytes 30752 | tf_op jit(solution)/shard_map/ppermute | solution.py:23
  73.3 1.2 %collective-permute-done.2 = bf16[4,8,32,15]{3,1,2,0:T(8,128)(2,1)S(1)} collective-permute-done((bf16[4,8,32,15]{3,1,2,0:T(8,128)(2,1)S(1)}, bf16[4,8,32,15]{3,1,2,0:T(8,128)(2,1)S(1)}, u32[]{:S(2)}, u32[]{:S(2)}) %collective-permute-start.2) | collective-permute-done | bytes 30752 | tf_op jit(solution)/shard_map/ppermute | solution.py:21
  74.5 0.3 pad_maximum_fusion.8
  74.8 0.6 convolution_bitcast_fusion.6
  75.4 0.7 convolution_bitcast_fusion.5
  76.1 0.8 fusion.10
  77.1 1.9 %collective-permute-start.5 = (bf16[8,32,15]{2,1,0:T(8,128)(2,1)S(1)}, bf16[8,32,15]{2,1,0:T(8,128)(2,1)S(1)}, u32[]{:S(2)}, u32[]{:S(2)}) collective-permute-start(bf16[8,32,15]{2,1,0:T(8,128)(2,1)S(1)} %get-tuple-element.10), channel_id=1, source_target_pairs={{1,0},{2,1},{3,2},{4,3},{5,4},{6,5},{7,6},{8,7},{9,8},{10,9},{11,1... | collective-permute-start | bytes 23048 | tf_op jit(solution)/shard_map/ppermute | solution.py:23
  79.0 4.6 %collective-permute-start.4 = (bf16[8,32,15]{2,1,0:T(8,128)(2,1)S(1)}, bf16[8,32,15]{2,1,0:T(8,128)(2,1)S(1)}, u32[]{:S(2)}, u32[]{:S(2)}) collective-permute-start(bf16[8,32,15]{2,1,0:T(8,128)(2,1)S(1)} %get-tuple-element.9), channel_id=1, source_target_pairs={{0,1},{1,2},{2,3},{3,4},{4,5},{5,6},{6,7},{7,8},{8,9},{9,10},{10,1... | collective-permute-start | bytes 23048 | tf_op jit(solution)/shard_map/ppermute | solution.py:21
  83.6 1.1 %collective-permute-done.4 = bf16[8,32,15]{2,1,0:T(8,128)(2,1)S(1)} collective-permute-done((bf16[8,32,15]{2,1,0:T(8,128)(2,1)S(1)}, bf16[8,32,15]{2,1,0:T(8,128)(2,1)S(1)}, u32[]{:S(2)}, u32[]{:S(2)}) %collective-permute-start.4) | collective-permute-done | bytes 7712 | tf_op jit(solution)/shard_map/ppermute | solution.py:21
  84.7 0.4 convolution_bitcast_fusion
  85.2 0.7 convolution_bitcast_fusion.4
  85.9 0.9 fusion.9
  86.8 0.1 fusion.76
  86.9 1.9 %collective-permute-start.7 = (bf16[4,8,32,15]{3,1,2,0:T(8,128)(2,1)S(1)}, bf16[4,8,32,15]{3,1,2,0:T(8,128)(2,1)S(1)}, u32[]{:S(2)}, u32[]{:S(2)}) collective-permute-start(bf16[4,8,32,15]{3,1,2,0:T(8,128)(2,1)S(1)} %get-tuple-element.6), channel_id=1, source_target_pairs={{1,0},{2,1},{3,2},{4,3},{5,4},{6,5},{7,6},{8,7},{9,8},{10,9},{11,1... | collective-permute-start | bytes 92168 | tf_op jit(solution)/shard_map/ppermute | solution.py:23
  88.8 4.3 %collective-permute-start.6 = (bf16[4,8,32,15]{3,1,2,0:T(8,128)(2,1)S(1)}, bf16[4,8,32,15]{3,1,2,0:T(8,128)(2,1)S(1)}, u32[]{:S(2)}, u32[]{:S(2)}) collective-permute-start(bf16[4,8,32,15]{3,1,2,0:T(8,128)(2,1)S(1)} %get-tuple-element.5), channel_id=1, source_target_pairs={{0,1},{1,2},{2,3},{3,4},{4,5},{5,6},{6,7},{7,8},{8,9},{9,10},{10,1... | collective-permute-start | bytes 92168 | tf_op jit(solution)/shard_map/ppermute | solution.py:21
  93.1 2.1 %collective-permute-done.7 = bf16[4,8,32,15]{3,1,2,0:T(8,128)(2,1)S(1)} collective-permute-done((bf16[4,8,32,15]{3,1,2,0:T(8,128)(2,1)S(1)}, bf16[4,8,32,15]{3,1,2,0:T(8,128)(2,1)S(1)}, u32[]{:S(2)}, u32[]{:S(2)}) %collective-permute-start.7) | collective-permute-done | bytes 30752 | tf_op jit(solution)/shard_map/ppermute | solution.py:23
  95.2 1.9 %collective-permute-done.6 = bf16[4,8,32,15]{3,1,2,0:T(8,128)(2,1)S(1)} collective-permute-done((bf16[4,8,32,15]{3,1,2,0:T(8,128)(2,1)S(1)}, bf16[4,8,32,15]{3,1,2,0:T(8,128)(2,1)S(1)}, u32[]{:S(2)}, u32[]{:S(2)}) %collective-permute-start.6) | collective-permute-done | bytes 30752 | tf_op jit(solution)/shard_map/ppermute | solution.py:21
  97.1 0.3 pad_maximum_fusion.9
  97.5 0.6 convolution_bitcast_fusion.3
  98.0 0.7 convolution_bitcast_fusion.2
  98.8 0.8 fusion.11
  99.6 0.7 fusion.46
  (27 shorter events, 0.6 us)
Async XLA Ops:
  6.3 13.8 %copy-start = (f32[8,32,128]{2,1,0:T(8,128)S(1)}, f32[8,32,128]{2,1,0:T(8,128)}, u32[]{:S(2)}) copy-start(f32[8,32,128]{2,1,0:T(8,128)} %param.6) | copy-start | bytes 393220
  6.3 19.6 %copy-start.1 = (f32[1,4,3,31]{3,1,2,0:T(4,128)S(1)}, f32[1,4,3,31]{3,1,2,0:T(4,128)}, u32[]{:S(2)}) copy-start(f32[1,4,3,31]{3,1,2,0:T(4,128)} %param.7) | copy-start | bytes 4468
  6.3 40.3 %copy-start.3 = (s32[16]{0:T(128)S(1)}, s32[16]{0:T(128)}, u32[]{:S(2)}) copy-start(s32[16]{0:T(128)} %param.8) | copy-start | bytes 196
  6.3 43.1 %copy-start.2 = (s32[16,4]{0,1:T(4,128)S(1)}, s32[16,4]{0,1:T(4,128)}, u32[]{:S(2)}) copy-start(s32[16,4]{0,1:T(4,128)} %param.9) | copy-start | bytes 772
  12.8 39.9 %all-to-all-start = ((bf16[16,2,4096]{2,1,0:T(2,128)(2,1)}), bf16[16,2,4096]{2,1,0:T(2,128)(2,1)S(1)}, u32[]{:S(2)}, u32[]{:S(2)}) async-start(bf16[16,2,4096]{2,1,0:T(2,128)(2,1)} %reshape.127), calls=%async_computation | async-start | bytes 524288 | tf_op jit(solution)/shard_map/all_to_all | solution.py:73
  20.3 31.2 %collective-permute-start.1 = (bf16[8,32,15]{2,1,0:T(8,128)(2,1)S(1)}, bf16[8,32,15]{2,1,0:T(8,128)(2,1)S(1)}, u32[]{:S(2)}, u32[]{:S(2)}) collective-permute-start(bf16[8,32,15]{2,1,0:T(8,128)(2,1)S(1)} %get-tuple-element.12), channel_id=1, source_target_pairs={{1,0},{2,1},{3,2},{4,3},{5,4},{6,5},{7,6},{8,7},{9,8},{10,9},{11,1... | collective-permute-start | bytes 23048 | tf_op jit(solution)/shard_map/ppermute | solution.py:23
  22.3 29.2 %collective-permute-start = (bf16[8,32,15]{2,1,0:T(8,128)(2,1)S(1)}, bf16[8,32,15]{2,1,0:T(8,128)(2,1)S(1)}, u32[]{:S(2)}, u32[]{:S(2)}) collective-permute-start(bf16[8,32,15]{2,1,0:T(8,128)(2,1)S(1)} %get-tuple-element.11), channel_id=1, source_target_pairs={{0,1},{1,2},{2,3},{3,4},{4,5},{5,6},{6,7},{7,8},{8,9},{9,10},{10,1... | collective-permute-start | bytes 23048 | tf_op jit(solution)/shard_map/ppermute | solution.py:21
  65.6 7.7 %collective-permute-start.3 = (bf16[4,8,32,15]{3,1,2,0:T(8,128)(2,1)S(1)}, bf16[4,8,32,15]{3,1,2,0:T(8,128)(2,1)S(1)}, u32[]{:S(2)}, u32[]{:S(2)}) collective-permute-start(bf16[4,8,32,15]{3,1,2,0:T(8,128)(2,1)S(1)} %get-tuple-element.8), channel_id=1, source_target_pairs={{1,0},{2,1},{3,2},{4,3},{5,4},{6,5},{7,6},{8,7},{9,8},{10,9},{11,1... | collective-permute-start | bytes 92168 | tf_op jit(solution)/shard_map/ppermute | solution.py:23
  67.7 6.8 %collective-permute-start.2 = (bf16[4,8,32,15]{3,1,2,0:T(8,128)(2,1)S(1)}, bf16[4,8,32,15]{3,1,2,0:T(8,128)(2,1)S(1)}, u32[]{:S(2)}, u32[]{:S(2)}) collective-permute-start(bf16[4,8,32,15]{3,1,2,0:T(8,128)(2,1)S(1)} %get-tuple-element.7), channel_id=1, source_target_pairs={{0,1},{1,2},{2,3},{3,4},{4,5},{5,6},{6,7},{7,8},{8,9},{9,10},{10,1... | collective-permute-start | bytes 92168 | tf_op jit(solution)/shard_map/ppermute | solution.py:21
  77.1 6.5 %collective-permute-start.5 = (bf16[8,32,15]{2,1,0:T(8,128)(2,1)S(1)}, bf16[8,32,15]{2,1,0:T(8,128)(2,1)S(1)}, u32[]{:S(2)}, u32[]{:S(2)}) collective-permute-start(bf16[8,32,15]{2,1,0:T(8,128)(2,1)S(1)} %get-tuple-element.10), channel_id=1, source_target_pairs={{1,0},{2,1},{3,2},{4,3},{5,4},{6,5},{7,6},{8,7},{9,8},{10,9},{11,1... | collective-permute-start | bytes 23048 | tf_op jit(solution)/shard_map/ppermute | solution.py:23
  79.0 5.7 %collective-permute-start.4 = (bf16[8,32,15]{2,1,0:T(8,128)(2,1)S(1)}, bf16[8,32,15]{2,1,0:T(8,128)(2,1)S(1)}, u32[]{:S(2)}, u32[]{:S(2)}) collective-permute-start(bf16[8,32,15]{2,1,0:T(8,128)(2,1)S(1)} %get-tuple-element.9), channel_id=1, source_target_pairs={{0,1},{1,2},{2,3},{3,4},{4,5},{5,6},{6,7},{7,8},{8,9},{9,10},{10,1... | collective-permute-start | bytes 23048 | tf_op jit(solution)/shard_map/ppermute | solution.py:21
  86.9 8.3 %collective-permute-start.7 = (bf16[4,8,32,15]{3,1,2,0:T(8,128)(2,1)S(1)}, bf16[4,8,32,15]{3,1,2,0:T(8,128)(2,1)S(1)}, u32[]{:S(2)}, u32[]{:S(2)}) collective-permute-start(bf16[4,8,32,15]{3,1,2,0:T(8,128)(2,1)S(1)} %get-tuple-element.6), channel_id=1, source_target_pairs={{1,0},{2,1},{3,2},{4,3},{5,4},{6,5},{7,6},{8,7},{9,8},{10,9},{11,1... | collective-permute-start | bytes 92168 | tf_op jit(solution)/shard_map/ppermute | solution.py:23
  88.8 8.3 %collective-permute-start.6 = (bf16[4,8,32,15]{3,1,2,0:T(8,128)(2,1)S(1)}, bf16[4,8,32,15]{3,1,2,0:T(8,128)(2,1)S(1)}, u32[]{:S(2)}, u32[]{:S(2)}) collective-permute-start(bf16[4,8,32,15]{3,1,2,0:T(8,128)(2,1)S(1)} %get-tuple-element.5), channel_id=1, source_target_pairs={{0,1},{1,2},{2,3},{3,4},{4,5},{5,6},{6,7},{7,8},{8,9},{9,10},{10,1... | collective-permute-start | bytes 92168 | tf_op jit(solution)/shard_map/ppermute | solution.py:21
where the time goes:
time: 101 us; the launch traced here: 100 us
  starting transfers between devices  31.2 us (31%)
  local copies, waits for them, and re-layouts  25.6 us (25%)
  blocking collectives  20.7 us (20%)
  matrix products  12.2 us (12%)
  waiting for transfers between devices  7.98 us (8%)
  other arithmetic  2.37 us (2%)
    all_gather x1, blocking collectives, shards(): fitted = lax.all_gather(psf_bank, ('plane', 'brick'), axis=0, tiled=True)  20.7 us
    unnamed x11, local copies, waits for them, and re-layouts  18.8 us
    ppermute x4, starting transfers between devices, padded_2(): lax.ppermute(tail, axis, [(i, (i + 1) % count) for i in range(ends)])  15.9 us
    ppermute x4, starting transfers between devices, padded_2(): lax.ppermute(head, axis, [((i + 1) % count, i) for i in range(ends)])  7.93 us
    all_to_all x1, starting transfers between devices, shards(): lax.all_to_all(camera_rows, ('plane', 'brick'), split_axis=3, concat_axis...  7.35 us
    convert_element_type x1, local copies, waits for them, and re-layouts, shards(): regrouped.astype(jnp.float32) / (blurred + BACKGROUND)  5.93 us
    ppermute x4, waiting for transfers between devices, padded_2(): lax.ppermute(tail, axis, [(i, (i + 1) % count) for i in range(ends)])  4.22 us
    ppermute x4, waiting for transfers between devices, padded_2(): lax.ppermute(head, axis, [((i + 1) % count, i) for i in range(ends)])  3.76 us
  transfers between devices with their start and end apart: 9, of which 5 were waited for; matrix products, arithmetic and copies ran while one was open for 7% of the time, Pallas kernels for 0%

commit v1 on v0

--- a/solution.py
+++ b/solution.py
@@ -8,6 +8,17 @@
 ITERS = 2
 BACKGROUND = 0.1
 HIGHEST = lax.Precision.HIGHEST
+
+
+def in_blocks(shard, dim, length):
+    before, after = (shard.shape[:dim], shard.shape[dim + 1 :])
+    return jnp.moveaxis(shard.reshape(*before, length, -1, *after), dim, 0)
+
+
+def laid_out(tiles, dim):
+    tiles = jnp.moveaxis(tiles, 0, dim)
+    dims = tiles.shape
+    return tiles.reshape(*dims[:dim], dims[dim] * dims[dim + 1], *dims[dim + 2 :])
 
 
 def padded_2(cells, sides, width):
@@ -70,9 +81,16 @@
 
 
 def shards(camera_rows, estimate, psf_bank, psf_owner, view_mask):
-    regrouped = lax.all_to_all(
-        camera_rows, ("plane", "brick"), split_axis=3, concat_axis=2, tiled=True
-    )
+    count_2, here = (lax.axis_size(("plane", "brick")), lax.axis_index(("plane", "brick")))
+    blocks = in_blocks(camera_rows, 3, count_2)
+    outs = [blocks[here]]
+    for step in range(1, count_2):
+        sent = blocks[here ^ step]
+        outs.append(
+            lax.ppermute(sent, ("plane", "brick"), [(i_2, i_2 ^ step) for i_2 in range(count_2)])
+        )
+    blocks = jnp.stack(outs)[here ^ jnp.arange(count_2)]
+    regrouped = laid_out(blocks, 2)
     position = lax.axis_index(("plane", "brick"))
     brick_ids = jnp.arange(psf_owner.shape[0], dtype=jnp.int32)
     is_mine = brick_ids == position

time: 101 us -> 98.2 us (0.972)
  local copies, waits for them, and re-layouts: 25.6 us -> 3.61 us
  starting transfers between devices: 31.2 us -> 41.1 us
  waiting for transfers between devices: 7.98 us -> 15.4 us
  blocking collectives: 20.7 us -> 22.3 us
    ppermute x0 -> x15, starting transfers between devices: none -> 21.4 us  [shards(): lax.ppermute(sent, ('plane', 'brick'), [(i_2, i_2 ^ step) for i_2 in rang...]
    unnamed x11 -> x38, local copies, waits for them, and re-layouts: 18.8 us -> 0.23 us
    ppermute x4, waiting for transfers between devices: 3.76 us -> 12 us  [padded_2(): lax.ppermute(head, axis, [((i + 1) % count, i) for i in range(ends)])]
    all_to_all x1 -> x0, starting transfers between devices: 7.35 us -> none  [shards(): lax.all_to_all(camera_rows, ('plane', 'brick'), split_axis=3, concat_axis...]
    convert_element_type x1, local copies, waits for them, and re-layouts: 5.93 us -> 0.04 us  [shards(): regrouped.astype(jnp.float32) / (blurred + BACKGROUND)]
    ppermute x4, starting transfers between devices: 15.9 us -> 10.8 us  [padded_2(): lax.ppermute(tail, axis, [(i, (i + 1) % count) for i in range(ends)])]
    ppermute x4, waiting for transfers between devices: 4.22 us -> 1.77 us  [padded_2(): lax.ppermute(tail, axis, [(i, (i + 1) % count) for i in range(ends)])]
    ppermute x0 -> x15, waiting for transfers between devices: none -> 1.66 us  [shards(): lax.ppermute(sent, ('plane', 'brick'), [(i_2, i_2 ^ step) for i_2 in rang...]
  transfers between devices with their start and end apart: 9 -> 23, of which waited for: 5 -> 7; matrix products, arithmetic and copies ran while one was open for 7% -> 7% of each run, Pallas kernels for 0% -> 0%
where the time goes in v1:
time: 98.2 us; the launch traced here: 97.7 us
  starting transfers between devices  41.1 us (42%)
  blocking collectives  22.3 us (23%)
  waiting for transfers between devices  15.4 us (16%)
  matrix products  12.2 us (12%)
  local copies, waits for them, and re-layouts  3.61 us (4%)
  other arithmetic  2.43 us (2%)
    all_gather x1, blocking collectives, shards(): fitted = lax.all_gather(psf_bank, ('plane', 'brick'), axis=0, tiled=True)  22.3 us
    ppermute x15, starting transfers between devices, shards(): lax.ppermute(sent, ('plane', 'brick'), [(i_2, i_2 ^ step) for i_2 in rang...  21.4 us
    ppermute x4, waiting for transfers between devices, padded_2(): lax.ppermute(head, axis, [((i + 1) % count, i) for i in range(ends)])  12 us
    ppermute x4, starting transfers between devices, padded_2(): lax.ppermute(tail, axis, [(i, (i + 1) % count) for i in range(ends)])  10.8 us
    ppermute x4, starting transfers between devices, padded_2(): lax.ppermute(head, axis, [((i + 1) % count, i) for i in range(ends)])  8.84 us
    dot_general x4, matrix products, across_depth(): return jnp.einsum('vzyc,vzw->vwyc', volume, band_z, precision=HIGHEST)  3.35 us
    dot_general x6, matrix products, banded(): return jnp.einsum('ijt,vt->vij', one_hot, profiles, precision=HIGHEST)  3.14 us
    dot_general x4, matrix products, across_rows(): result = jnp.einsum('vzqic,vij->vzqjc', windows, band_y, precision=HIGHEST)  2.82 us
  transfers between devices with their start and end apart: 23, of which 7 were waited for; matrix products, arithmetic and copies ran while one was open for 7% of the time, Pallas kernels for 0%

profile of v1, /device:TPU:1, one launch (start us, length us, event | category | flops | bytes accessed | tf_op | source)
XLA Modules:
  0.0 97.7 jit_solution(2223158710586425879)
XLA Ops:
  0.0 1.1 %reshape.184 = bf16[4,8,2,16,128]{4,3,2,1,0:T(8,128)(2,1)S(1)} reshape(bf16[4,8,2,2048]{3,2,1,0:T(2,128)(2,1)} %param.5) | data formatting | bytes 524288 | tf_op jit(solution)/shard_map/reshape | solution.py:15
  1.2 0.7 constant_dynamic-slice_fusion
  2.1 2.7 %collective-permute-start.1 = (bf16[4,8,2,128]{3,1,2,0:T(8,128)(2,1)S(1)}, bf16[4,8,2,128]{3,1,2,0:T(8,128)(2,1)S(1)}, u32[]{:S(2)}, u32[]{:S(2)}) collective-permute-start(bf16[4,8,2,128]{3,1,2,0:T(8,128)(2,1)S(1)} %bitcast.218), channel_id=1, source_target_pairs={{0,2},{1,3},{2,0},{3,1},{4,6},{5,7},{6,4},{7,5},{8,10},{9,11},{10,... | collective-permute-start | bytes 49160 | tf_op jit(solution)/shard_map/ppermute | solution.py:90
  5.0 3.6 %collective-permute-start.15 = (bf16[8,32,15]{2,1,0:T(8,128)(2,1)S(1)}, bf16[8,32,15]{2,1,0:T(8,128)(2,1)S(1)}, u32[]{:S(2)}, u32[]{:S(2)}) collective-permute-start(bf16[8,32,15]{2,1,0:T(8,128)(2,1)S(1)} %get-tuple-element.27), channel_id=1, source_target_pairs={{0,1},{1,2},{2,3},{3,4},{4,5},{5,6},{6,7},{7,8},{8,9},{9,10},{10,1... | collective-permute-start | bytes 23048 | tf_op jit(solution)/shard_map/ppermute | solution.py:32
  8.6 1.9 %collective-permute-start.16 = (bf16[8,32,15]{2,1,0:T(8,128)(2,1)S(1)}, bf16[8,32,15]{2,1,0:T(8,128)(2,1)S(1)}, u32[]{:S(2)}, u32[]{:S(2)}) collective-permute-start(bf16[8,32,15]{2,1,0:T(8,128)(2,1)S(1)} %get-tuple-element.28), channel_id=1, source_target_pairs={{1,0},{2,1},{3,2},{4,3},{5,4},{6,5},{7,6},{8,7},{9,8},{10,9},{11,1... | collective-permute-start | bytes 23048 | tf_op jit(solution)/shard_map/ppermute | solution.py:34
  10.6 0.6 select_reduce_fusion.1
  11.2 22.3 %all_gather.3 = f32[16,4,3,31]{3,1,2,0:T(4,128)S(1)} all-gather(f32[1,4,3,31]{3,1,2,0:T(4,128)S(1)} %copy-done.1), channel_id=1, replica_groups=mesh['slab'=2,'plane'=8,'brick'=2] {'plane','brick'}, dimensions={0}, use_global_device_ids=true | all-gather | bytes 25296 | tf_op jit(solution)/shard_map/all_gather | solution.py:99
  33.6 0.8 fusion.48
  34.5 0.9 fusion.12
  35.4 0.3 convolution_bitcast_fusion.8
  35.7 0.4 convolution_bitcast_fusion.10
  36.3 0.9 fusion.13
  38.0 1.8 %collective-permute-start.4 = (bf16[4,8,2,128]{3,1,2,0:T(8,128)(2,1)S(1)}, bf16[4,8,2,128]{3,1,2,0:T(8,128)(2,1)S(1)}, u32[]{:S(2)}, u32[]{:S(2)}) collective-permute-start(bf16[4,8,2,128]{3,1,2,0:T(8,128)(2,1)S(1)} %bitcast.223), channel_id=1, source_target_pairs={{0,5},{1,4},{2,7},{3,6},{4,1},{5,0},{6,3},{7,2},{8,13},{9,12},{10,... | collective-permute-start | bytes 49160 | tf_op jit(solution)/shard_map/ppermute | solution.py:90
  39.8 0.4 convolution_bitcast_fusion.1
  40.3 0.7 convolution_bitcast_fusion.7
  41.1 2.6 %collective-permute-start.6 = (bf16[4,8,2,128]{3,1,2,0:T(8,128)(2,1)S(1)}, bf16[4,8,2,128]{3,1,2,0:T(8,128)(2,1)S(1)}, u32[]{:S(2)}, u32[]{:S(2)}) collective-permute-start(bf16[4,8,2,128]{3,1,2,0:T(8,128)(2,1)S(1)} %bitcast.221), channel_id=1, source_target_pairs={{0,7},{1,6},{2,5},{3,4},{4,3},{5,2},{6,1},{7,0},{8,15},{9,14},{10,... | collective-permute-start | bytes 49160 | tf_op jit(solution)/shard_map/ppermute | solution.py:90
  43.7 2.7 %collective-permute-start.8 = (bf16[4,8,2,128]{3,1,2,0:T(8,128)(2,1)S(1)}, bf16[4,8,2,128]{3,1,2,0:T(8,128)(2,1)S(1)}, u32[]{:S(2)}, u32[]{:S(2)}) collective-permute-start(bf16[4,8,2,128]{3,1,2,0:T(8,128)(2,1)S(1)} %bitcast.217), channel_id=1, source_target_pairs={{0,9},{1,8},{2,11},{3,10},{4,13},{5,12},{6,15},{7,14},{8,1},{9,0},... | collective-permute-start | bytes 49160 | tf_op jit(solution)/shard_map/ppermute | solution.py:90
  46.4 3.5 %collective-permute-start.10 = (bf16[4,8,2,128]{3,1,2,0:T(8,128)(2,1)S(1)}, bf16[4,8,2,128]{3,1,2,0:T(8,128)(2,1)S(1)}, u32[]{:S(2)}, u32[]{:S(2)}) collective-permute-start(bf16[4,8,2,128]{3,1,2,0:T(8,128)(2,1)S(1)} %bitcast.214), channel_id=1, source_target_pairs={{0,11},{1,10},{2,9},{3,8},{4,15},{5,14},{6,13},{7,12},{8,3},{9,2},... | collective-permute-start | bytes 49160 | tf_op jit(solution)/shard_map/ppermute | solution.py:90
  49.9 3.6 %collective-permute-start.12 = (bf16[4,8,2,128]{3,1,2,0:T(8,128)(2,1)S(1)}, bf16[4,8,2,128]{3,1,2,0:T(8,128)(2,1)S(1)}, u32[]{:S(2)}, u32[]{:S(2)}) collective-permute-start(bf16[4,8,2,128]{3,1,2,0:T(8,128)(2,1)S(1)} %bitcast.212), channel_id=1, source_target_pairs={{0,13},{1,12},{2,15},{3,14},{4,9},{5,8},{6,11},{7,10},{8,5},{9,4},... | collective-permute-start | bytes 49160 | tf_op jit(solution)/shard_map/ppermute | solution.py:90
  53.6 4.4 %collective-permute-start.14 = (bf16[4,8,2,128]{3,1,2,0:T(8,128)(2,1)S(1)}, bf16[4,8,2,128]{3,1,2,0:T(8,128)(2,1)S(1)}, u32[]{:S(2)}, u32[]{:S(2)}) collective-permute-start(bf16[4,8,2,128]{3,1,2,0:T(8,128)(2,1)S(1)} %bitcast.210), channel_id=1, source_target_pairs={{0,15},{1,14},{2,13},{3,12},{4,11},{5,10},{6,9},{7,8},{8,7},{9,6},... | collective-permute-start | bytes 49160 | tf_op jit(solution)/shard_map/ppermute | solution.py:90
  58.0 0.8 collective-permute-done.13
  58.8 0.8 collective-permute-done.14
  59.6 0.6 gather_fusion
  60.3 0.9 fusion.8
  61.4 3.4 %collective-permute-start.17 = (bf16[4,8,32,15]{3,1,2,0:T(8,128)(2,1)S(1)}, bf16[4,8,32,15]{3,1,2,0:T(8,128)(2,1)S(1)}, u32[]{:S(2)}, u32[]{:S(2)}) collective-permute-start(bf16[4,8,32,15]{3,1,2,0:T(8,128)(2,1)S(1)} %get-tuple-element.7), channel_id=1, source_target_pairs={{0,1},{1,2},{2,3},{3,4},{4,5},{5,6},{6,7},{7,8},{8,9},{9,10},{10,1... | collective-permute-start | bytes 92168 | tf_op jit(solution)/shard_map/ppermute | solution.py:32
  64.7 1.9 %collective-permute-start.18 = (bf16[4,8,32,15]{3,1,2,0:T(8,128)(2,1)S(1)}, bf16[4,8,32,15]{3,1,2,0:T(8,128)(2,1)S(1)}, u32[]{:S(2)}, u32[]{:S(2)}) collective-permute-start(bf16[4,8,32,15]{3,1,2,0:T(8,128)(2,1)S(1)} %get-tuple-element.8), channel_id=1, source_target_pairs={{1,0},{2,1},{3,2},{4,3},{5,4},{6,5},{7,6},{8,7},{9,8},{10,9},{11,1... | collective-permute-start | bytes 92168 | tf_op jit(solution)/shard_map/ppermute | solution.py:34
  66.6 0.4 convolution_bitcast_fusion.11
  67.1 0.9 collective-permute-done.17
  68.0 4.4 %collective-permute-done.18 = bf16[4,8,32,15]{3,1,2,0:T(8,128)(2,1)S(1)} collective-permute-done((bf16[4,8,32,15]{3,1,2,0:T(8,128)(2,1)S(1)}, bf16[4,8,32,15]{3,1,2,0:T(8,128)(2,1)S(1)}, u32[]{:S(2)}, u32[]{:S(2)}) %collective-permute-start.18) | collective-permute-done | bytes 30752 | tf_op jit(solution)/shard_map/ppermute | solution.py:34
  72.4 0.3 pad_maximum_fusion.8
  72.7 0.6 convolution_bitcast_fusion.6
  73.3 0.7 convolution_bitcast_fusion.5
  74.0 0.8 fusion.10
  75.0 1.9 %collective-permute-start.19 = (bf16[8,32,15]{2,1,0:T(8,128)(2,1)S(1)}, bf16[8,32,15]{2,1,0:T(8,128)(2,1)S(1)}, u32[]{:S(2)}, u32[]{:S(2)}) collective-permute-start(bf16[8,32,15]{2,1,0:T(8,128)(2,1)S(1)} %get-tuple-element.25), channel_id=1, source_target_pairs={{0,1},{1,2},{2,3},{3,4},{4,5},{5,6},{6,7},{7,8},{8,9},{9,10},{10,1... | collective-permute-start | bytes 23048 | tf_op jit(solution)/shard_map/ppermute | solution.py:32
  76.9 2.6 %collective-permute-start.20 = (bf16[8,32,15]{2,1,0:T(8,128)(2,1)S(1)}, bf16[8,32,15]{2,1,0:T(8,128)(2,1)S(1)}, u32[]{:S(2)}, u32[]{:S(2)}) collective-permute-start(bf16[8,32,15]{2,1,0:T(8,128)(2,1)S(1)} %get-tuple-element.26), channel_id=1, source_target_pairs={{1,0},{2,1},{3,2},{4,3},{5,4},{6,5},{7,6},{8,7},{9,8},{10,9},{11,1... | collective-permute-start | bytes 23048 | tf_op jit(solution)/shard_map/ppermute | solution.py:34
  79.5 3.0 %collective-permute-done.20 = bf16[8,32,15]{2,1,0:T(8,128)(2,1)S(1)} collective-permute-done((bf16[8,32,15]{2,1,0:T(8,128)(2,1)S(1)}, bf16[8,32,15]{2,1,0:T(8,128)(2,1)S(1)}, u32[]{:S(2)}, u32[]{:S(2)}) %collective-permute-start.20) | collective-permute-done | bytes 7712 | tf_op jit(solution)/shard_map/ppermute | solution.py:34
  82.5 0.4 convolution_bitcast_fusion
  83.0 0.7 convolution_bitcast_fusion.4
  83.7 0.9 fusion.9
  84.7 1.9 %collective-permute-start.21 = (bf16[4,8,32,15]{3,1,2,0:T(8,128)(2,1)S(1)}, bf16[4,8,32,15]{3,1,2,0:T(8,128)(2,1)S(1)}, u32[]{:S(2)}, u32[]{:S(2)}) collective-permute-start(bf16[4,8,32,15]{3,1,2,0:T(8,128)(2,1)S(1)} %get-tuple-element.5), channel_id=1, source_target_pairs={{0,1},{1,2},{2,3},{3,4},{4,5},{5,6},{6,7},{7,8},{8,9},{9,10},{10,1... | collective-permute-start | bytes 92168 | tf_op jit(solution)/shard_map/ppermute | solution.py:32
  86.6 2.4 %collective-permute-start.22 = (bf16[4,8,32,15]{3,1,2,0:T(8,128)(2,1)S(1)}, bf16[4,8,32,15]{3,1,2,0:T(8,128)(2,1)S(1)}, u32[]{:S(2)}, u32[]{:S(2)}) collective-permute-start(bf16[4,8,32,15]{3,1,2,0:T(8,128)(2,1)S(1)} %get-tuple-element.6), channel_id=1, source_target_pairs={{1,0},{2,1},{3,2},{4,3},{5,4},{6,5},{7,6},{8,7},{9,8},{10,9},{11,1... | collective-permute-start | bytes 92168 | tf_op jit(solution)/shard_map/ppermute | solution.py:34
  89.0 0.9 collective-permute-done.21
  89.9 4.6 %collective-permute-done.22 = bf16[4,8,32,15]{3,1,2,0:T(8,128)(2,1)S(1)} collective-permute-done((bf16[4,8,32,15]{3,1,2,0:T(8,128)(2,1)S(1)}, bf16[4,8,32,15]{3,1,2,0:T(8,128)(2,1)S(1)}, u32[]{:S(2)}, u32[]{:S(2)}) %collective-permute-start.22) | collective-permute-done | bytes 30752 | tf_op jit(solution)/shard_map/ppermute | solution.py:34
  94.5 0.3 pad_maximum_fusion.9
  94.8 0.6 convolution_bitcast_fusion.3
  95.4 0.7 convolution_bitcast_fusion.2
  96.1 0.8 fusion.11
  96.9 0.7 fusion.46
  (89 shorter events, 2.2 us)
Async XLA Ops:
  1.2 3.6 %copy-start = (f32[8,32,128]{2,1,0:T(8,128)S(1)}, f32[8,32,128]{2,1,0:T(8,128)}, u32[]{:S(2)}) copy-start(f32[8,32,128]{2,1,0:T(8,128)} %param.6) | copy-start | bytes 393220
  1.9 8.7 %copy-start.3 = (s32[16]{0:T(128)S(1)}, s32[16]{0:T(128)}, u32[]{:S(2)}) copy-start(s32[16]{0:T(128)} %param.8) | copy-start | bytes 196
  1.9 9.3 %copy-start.1 = (f32[1,4,3,31]{3,1,2,0:T(4,128)S(1)}, f32[1,4,3,31]{3,1,2,0:T(4,128)}, u32[]{:S(2)}) copy-start(f32[1,4,3,31]{3,1,2,0:T(4,128)} %param.7) | copy-start | bytes 4468
  2.0 39.0 %collective-permute-start = (bf16[4,8,2,128]{3,1,2,0:T(8,128)(2,1)S(1)}, bf16[4,8,2,128]{3,1,2,0:T(8,128)(2,1)S(1)}, u32[]{:S(2)}, u32[]{:S(2)}) collective-permute-start(bf16[4,8,2,128]{3,1,2,0:T(8,128)(2,1)S(1)} %bitcast.219), channel_id=1, source_target_pairs={{0,1},{1,0},{2,3},{3,2},{4,5},{5,4},{6,7},{7,6},{8,9},{9,8},{10,11... | collective-permute-start | bytes 49160 | tf_op jit(solution)/shard_map/ppermute | solution.py:90
  2.1 39.0 %collective-permute-start.1 = (bf16[4,8,2,128]{3,1,2,0:T(8,128)(2,1)S(1)}, bf16[4,8,2,128]{3,1,2,0:T(8,128)(2,1)S(1)}, u32[]{:S(2)}, u32[]{:S(2)}) collective-permute-start(bf16[4,8,2,128]{3,1,2,0:T(8,128)(2,1)S(1)} %bitcast.218), channel_id=1, source_target_pairs={{0,2},{1,3},{2,0},{3,1},{4,6},{5,7},{6,4},{7,5},{8,10},{9,11},{10,... | collective-permute-start | bytes 49160 | tf_op jit(solution)/shard_map/ppermute | solution.py:90
  4.8 38.9 %collective-permute-start.2 = (bf16[4,8,2,128]{3,1,2,0:T(8,128)(2,1)S(1)}, bf16[4,8,2,128]{3,1,2,0:T(8,128)(2,1)S(1)}, u32[]{:S(2)}, u32[]{:S(2)}) collective-permute-start(bf16[4,8,2,128]{3,1,2,0:T(8,128)(2,1)S(1)} %bitcast.216), channel_id=1, source_target_pairs={{0,3},{1,2},{2,1},{3,0},{4,7},{5,6},{6,5},{7,4},{8,11},{9,10},{10,... | collective-permute-start | bytes 49160 | tf_op jit(solution)/shard_map/ppermute | solution.py:90
  5.0 33.0 %collective-permute-start.15 = (bf16[8,32,15]{2,1,0:T(8,128)(2,1)S(1)}, bf16[8,32,15]{2,1,0:T(8,128)(2,1)S(1)}, u32[]{:S(2)}, u32[]{:S(2)}) collective-permute-start(bf16[8,32,15]{2,1,0:T(8,128)(2,1)S(1)} %get-tuple-element.27), channel_id=1, source_target_pairs={{0,1},{1,2},{2,3},{3,4},{4,5},{5,6},{6,7},{7,8},{8,9},{9,10},{10,1... | collective-permute-start | bytes 23048 | tf_op jit(solution)/shard_map/ppermute | solution.py:32
  8.6 29.4 %collective-permute-start.16 = (bf16[8,32,15]{2,1,0:T(8,128)(2,1)S(1)}, bf16[8,32,15]{2,1,0:T(8,128)(2,1)S(1)}, u32[]{:S(2)}, u32[]{:S(2)}) collective-permute-start(bf16[8,32,15]{2,1,0:T(8,128)(2,1)S(1)} %get-tuple-element.28), channel_id=1, source_target_pairs={{1,0},{2,1},{3,2},{4,3},{5,4},{6,5},{7,6},{8,7},{9,8},{10,9},{11,1... | collective-permute-start | bytes 23048 | tf_op jit(solution)/shard_map/ppermute | solution.py:34
  10.6 25.5 %copy-start.2 = (s32[16,4]{0,1:T(4,128)S(1)}, s32[16,4]{0,1:T(4,128)}, u32[]{:S(2)}) copy-start(s32[16,4]{0,1:T(4,128)} %param.9) | copy-start | bytes 772
  38.0 5.7 %collective-permute-start.3 = (bf16[4,8,2,128]{3,1,2,0:T(8,128)(2,1)S(1)}, bf16[4,8,2,128]{3,1,2,0:T(8,128)(2,1)S(1)}, u32[]{:S(2)}, u32[]{:S(2)}) collective-permute-start(bf16[4,8,2,128]{3,1,2,0:T(8,128)(2,1)S(1)} %bitcast.224), channel_id=1, source_target_pairs={{0,4},{1,5},{2,6},{3,7},{4,0},{5,1},{6,2},{7,3},{8,12},{9,13},{10,... | collective-permute-start | bytes 49160 | tf_op jit(solution)/shard_map/ppermute | solution.py:90
  38.0 8.4 %collective-permute-start.4 = (bf16[4,8,2,128]{3,1,2,0:T(8,128)(2,1)S(1)}, bf16[4,8,2,128]{3,1,2,0:T(8,128)(2,1)S(1)}, u32[]{:S(2)}, u32[]{:S(2)}) collective-permute-start(bf16[4,8,2,128]{3,1,2,0:T(8,128)(2,1)S(1)} %bitcast.223), channel_id=1, source_target_pairs={{0,5},{1,4},{2,7},{3,6},{4,1},{5,0},{6,3},{7,2},{8,13},{9,12},{10,... | collective-permute-start | bytes 49160 | tf_op jit(solution)/shard_map/ppermute | solution.py:90
  41.0 5.4 %collective-permute-start.5 = (bf16[4,8,2,128]{3,1,2,0:T(8,128)(2,1)S(1)}, bf16[4,8,2,128]{3,1,2,0:T(8,128)(2,1)S(1)}, u32[]{:S(2)}, u32[]{:S(2)}) collective-permute-start(bf16[4,8,2,128]{3,1,2,0:T(8,128)(2,1)S(1)} %bitcast.222), channel_id=1, source_target_pairs={{0,6},{1,7},{2,4},{3,5},{4,2},{5,3},{6,0},{7,1},{8,14},{9,15},{10,... | collective-permute-start | bytes 49160 | tf_op jit(solution)/shard_map/ppermute | solution.py:90
  41.1 8.8 %collective-permute-start.6 = (bf16[4,8,2,128]{3,1,2,0:T(8,128)(2,1)S(1)}, bf16[4,8,2,128]{3,1,2,0:T(8,128)(2,1)S(1)}, u32[]{:S(2)}, u32[]{:S(2)}) collective-permute-start(bf16[4,8,2,128]{3,1,2,0:T(8,128)(2,1)S(1)} %bitcast.221), channel_id=1, source_target_pairs={{0,7},{1,6},{2,5},{3,4},{4,3},{5,2},{6,1},{7,0},{8,15},{9,14},{10,... | collective-permute-start | bytes 49160 | tf_op jit(solution)/shard_map/ppermute | solution.py:90
  43.7 6.3 %collective-permute-start.7 = (bf16[4,8,2,128]{3,1,2,0:T(8,128)(2,1)S(1)}, bf16[4,8,2,128]{3,1,2,0:T(8,128)(2,1)S(1)}, u32[]{:S(2)}, u32[]{:S(2)}) collective-permute-start(bf16[4,8,2,128]{3,1,2,0:T(8,128)(2,1)S(1)} %bitcast.220), channel_id=1, source_target_pairs={{0,8},{1,9},{2,10},{3,11},{4,12},{5,13},{6,14},{7,15},{8,0},{9,1},... | collective-permute-start | bytes 49160 | tf_op jit(solution)/shard_map/ppermute | solution.py:90
  43.7 9.8 %collective-permute-start.8 = (bf16[4,8,2,128]{3,1,2,0:T(8,128)(2,1)S(1)}, bf16[4,8,2,128]{3,1,2,0:T(8,128)(2,1)S(1)}, u32[]{:S(2)}, u32[]{:S(2)}) collective-permute-start(bf16[4,8,2,128]{3,1,2,0:T(8,128)(2,1)S(1)} %bitcast.217), channel_id=1, source_target_pairs={{0,9},{1,8},{2,11},{3,10},{4,13},{5,12},{6,15},{7,14},{8,1},{9,0},... | collective-permute-start | bytes 49160 | tf_op jit(solution)/shard_map/ppermute | solution.py:90
  46.4 7.2 %collective-permute-start.9 = (bf16[4,8,2,128]{3,1,2,0:T(8,128)(2,1)S(1)}, bf16[4,8,2,128]{3,1,2,0:T(8,128)(2,1)S(1)}, u32[]{:S(2)}, u32[]{:S(2)}) collective-permute-start(bf16[4,8,2,128]{3,1,2,0:T(8,128)(2,1)S(1)} %bitcast.215), channel_id=1, source_target_pairs={{0,10},{1,11},{2,8},{3,9},{4,14},{5,15},{6,12},{7,13},{8,2},{9,3},... | collective-permute-start | bytes 49160 | tf_op jit(solution)/shard_map/ppermute | solution.py:90
  46.4 11.5 %collective-permute-start.10 = (bf16[4,8,2,128]{3,1,2,0:T(8,128)(2,1)S(1)}, bf16[4,8,2,128]{3,1,2,0:T(8,128)(2,1)S(1)}, u32[]{:S(2)}, u32[]{:S(2)}) collective-permute-start(bf16[4,8,2,128]{3,1,2,0:T(8,128)(2,1)S(1)} %bitcast.214), channel_id=1, source_target_pairs={{0,11},{1,10},{2,9},{3,8},{4,15},{5,14},{6,13},{7,12},{8,3},{9,2},... | collective-permute-start | bytes 49160 | tf_op jit(solution)/shard_map/ppermute | solution.py:90
  49.9 8.0 %collective-permute-start.11 = (bf16[4,8,2,128]{3,1,2,0:T(8,128)(2,1)S(1)}, bf16[4,8,2,128]{3,1,2,0:T(8,128)(2,1)S(1)}, u32[]{:S(2)}, u32[]{:S(2)}) collective-permute-start(bf16[4,8,2,128]{3,1,2,0:T(8,128)(2,1)S(1)} %bitcast.213), channel_id=1, source_target_pairs={{0,12},{1,13},{2,14},{3,15},{4,8},{5,9},{6,10},{7,11},{8,4},{9,5},... | collective-permute-start | bytes 49160 | tf_op jit(solution)/shard_map/ppermute | solution.py:90
  49.9 8.0 %collective-permute-start.12 = (bf16[4,8,2,128]{3,1,2,0:T(8,128)(2,1)S(1)}, bf16[4,8,2,128]{3,1,2,0:T(8,128)(2,1)S(1)}, u32[]{:S(2)}, u32[]{:S(2)}) collective-permute-start(bf16[4,8,2,128]{3,1,2,0:T(8,128)(2,1)S(1)} %bitcast.212), channel_id=1, source_target_pairs={{0,13},{1,12},{2,15},{3,14},{4,9},{5,8},{6,11},{7,10},{8,5},{9,4},... | collective-permute-start | bytes 49160 | tf_op jit(solution)/shard_map/ppermute | solution.py:90
  53.5 5.3 %collective-permute-start.13 = (bf16[4,8,2,128]{3,1,2,0:T(8,128)(2,1)S(1)}, bf16[4,8,2,128]{3,1,2,0:T(8,128)(2,1)S(1)}, u32[]{:S(2)}, u32[]{:S(2)}) collective-permute-start(bf16[4,8,2,128]{3,1,2,0:T(8,128)(2,1)S(1)} %bitcast.211), channel_id=1, source_target_pairs={{0,14},{1,15},{2,12},{3,13},{4,10},{5,11},{6,8},{7,9},{8,6},{9,7},... | collective-permute-start | bytes 49160 | tf_op jit(solution)/shard_map/ppermute | solution.py:90
  53.6 6.1 %collective-permute-start.14 = (bf16[4,8,2,128]{3,1,2,0:T(8,128)(2,1)S(1)}, bf16[4,8,2,128]{3,1,2,0:T(8,128)(2,1)S(1)}, u32[]{:S(2)}, u32[]{:S(2)}) collective-permute-start(bf16[4,8,2,128]{3,1,2,0:T(8,128)(2,1)S(1)} %bitcast.210), channel_id=1, source_target_pairs={{0,15},{1,14},{2,13},{3,12},{4,11},{5,10},{6,9},{7,8},{8,7},{9,6},... | collective-permute-start | bytes 49160 | tf_op jit(solution)/shard_map/ppermute | solution.py:90
  61.4 6.7 %collective-permute-start.17 = (bf16[4,8,32,15]{3,1,2,0:T(8,128)(2,1)S(1)}, bf16[4,8,32,15]{3,1,2,0:T(8,128)(2,1)S(1)}, u32[]{:S(2)}, u32[]{:S(2)}) collective-permute-start(bf16[4,8,32,15]{3,1,2,0:T(8,128)(2,1)S(1)} %get-tuple-element.7), channel_id=1, source_target_pairs={{0,1},{1,2},{2,3},{3,4},{4,5},{5,6},{6,7},{7,8},{8,9},{9,10},{10,1... | collective-permute-start | bytes 92168 | tf_op jit(solution)/shard_map/ppermute | solution.py:32
  64.7 7.7 %collective-permute-start.18 = (bf16[4,8,32,15]{3,1,2,0:T(8,128)(2,1)S(1)}, bf16[4,8,32,15]{3,1,2,0:T(8,128)(2,1)S(1)}, u32[]{:S(2)}, u32[]{:S(2)}) collective-permute-start(bf16[4,8,32,15]{3,1,2,0:T(8,128)(2,1)S(1)} %get-tuple-element.8), channel_id=1, source_target_pairs={{1,0},{2,1},{3,2},{4,3},{5,4},{6,5},{7,6},{8,7},{9,8},{10,9},{11,1... | collective-permute-start | bytes 92168 | tf_op jit(solution)/shard_map/ppermute | solution.py:34
  75.0 4.5 %collective-permute-start.19 = (bf16[8,32,15]{2,1,0:T(8,128)(2,1)S(1)}, bf16[8,32,15]{2,1,0:T(8,128)(2,1)S(1)}, u32[]{:S(2)}, u32[]{:S(2)}) collective-permute-start(bf16[8,32,15]{2,1,0:T(8,128)(2,1)S(1)} %get-tuple-element.25), channel_id=1, source_target_pairs={{0,1},{1,2},{2,3},{3,4},{4,5},{5,6},{6,7},{7,8},{8,9},{9,10},{10,1... | collective-permute-start | bytes 23048 | tf_op jit(solution)/shard_map/ppermute | solution.py:32
  76.9 5.6 %collective-permute-start.20 = (bf16[8,32,15]{2,1,0:T(8,128)(2,1)S(1)}, bf16[8,32,15]{2,1,0:T(8,128)(2,1)S(1)}, u32[]{:S(2)}, u32[]{:S(2)}) collective-permute-start(bf16[8,32,15]{2,1,0:T(8,128)(2,1)S(1)} %get-tuple-element.26), channel_id=1, source_target_pairs={{1,0},{2,1},{3,2},{4,3},{5,4},{6,5},{7,6},{8,7},{9,8},{10,9},{11,1... | collective-permute-start | bytes 23048 | tf_op jit(solution)/shard_map/ppermute | solution.py:34
  84.7 5.2 %collective-permute-start.21 = (bf16[4,8,32,15]{3,1,2,0:T(8,128)(2,1)S(1)}, bf16[4,8,32,15]{3,1,2,0:T(8,128)(2,1)S(1)}, u32[]{:S(2)}, u32[]{:S(2)}) collective-permute-start(bf16[4,8,32,15]{3,1,2,0:T(8,128)(2,1)S(1)} %get-tuple-element.5), channel_id=1, source_target_pairs={{0,1},{1,2},{2,3},{3,4},{4,5},{5,6},{6,7},{7,8},{8,9},{9,10},{10,1... | collective-permute-start | bytes 92168 | tf_op jit(solution)/shard_map/ppermute | solution.py:32
  86.6 7.9 %collective-permute-start.22 = (bf16[4,8,32,15]{3,1,2,0:T(8,128)(2,1)S(1)}, bf16[4,8,32,15]{3,1,2,0:T(8,128)(2,1)S(1)}, u32[]{:S(2)}, u32[]{:S(2)}) collective-permute-start(bf16[4,8,32,15]{3,1,2,0:T(8,128)(2,1)S(1)} %get-tuple-element.6), channel_id=1, source_target_pairs={{1,0},{2,1},{3,2},{4,3},{5,4},{6,5},{7,6},{8,7},{9,8},{10,9},{11,1... | collective-permute-start | bytes 92168 | tf_op jit(solution)/shard_map/ppermute | solution.py:34
